TPU v7x, 32 devices: a whole 2x2x4 slice. The times are simulated.
32 devices in a mesh: bubble: 8 (over z, y), panel: 4 (over x, core).
Axes of the slice: x: 2, y: 2, z: 4, core: 2. Of those that a mesh axis runs over, the one named last changes fastest.
Arguments:
- density: float32 [64, 12288], P('bubble', 'panel'), may hold values from -6 to 6
- right_side: float32 [64, 12288], P('bubble', 'panel'), may hold values from -6 to 6
- inv_diag: bfloat16 [64, 96, 128, 128], P('bubble', 'panel')
- near_vals: bfloat16 [64, 96, 4, 128, 128], P('bubble', 'panel'), may hold values from -0.25 to 0.25
- near_bubble: int32 [64, 96, 4], P('bubble', 'panel'), may hold values from 0 to 63, as said below
- near_block: int32 [64, 96, 4], P('bubble', 'panel'), may hold values from 0 to 95
- near_count: int32 [64, 96], P('bubble', 'panel'), may hold values from 1 to 4, as said below
- colour: int32 [64], P('bubble'), may hold values from 0 to 1
- moment_map: bfloat16 [64, 16, 12288], P('bubble', None, 'panel'), may hold values from -0.0546875 to 0.0546875
- spread_map: bfloat16 [64, 16, 12288], P('bubble', None, 'panel'), may hold values from -0.1875 to 0.1875
- centres: float32 [3, 64], replicated, may hold values from 0.2 to 6
Outputs:
- relaxed: float32 [64, 12288], P('bubble', 'panel')
Inputs may be any that keep to these rules, and one draw needn't show every extreme that they name: `near_bubble`: every slot of bubble b names a bubble within 8 of b. `near_count`: the first row block of every bubble uses all 4 slots.
All inputs are finite; a program needn't handle non-finite values.
Results may differ from a plain program's by a relative error of at most 0.0041.
Values may be sent and summed in bfloat16 or wider, within the bound.
A program may use at most 64 MiB of HBM per device.

v0:
```python
import jax
import jax.numpy as jnp
from jax import lax
from jax.sharding import PartitionSpec as P


def with_halo(shard, sides, width):
    for axis, dim in sides:
        peers, length = (lax.axis_size(axis), shard.shape[dim])
        up = [(i, (i + 1) % peers) for i in range(peers - 1)]
        down = [(j, i) for i, j in up]
        last = lax.slice_in_dim(shard, length - width, length, axis=dim)
        first = lax.slice_in_dim(shard, 0, width, axis=dim)
        before = lax.ppermute(last, axis, up)
        after = lax.ppermute(first, axis, down)
        shard = jnp.concatenate([before, shard, after], axis=dim)
    return shard


def near_field(
    neighbourhood, near_vals, near_bubble, near_block, near_count, first_bubble, block_size
):
    rim_count = neighbourhood.shape[0]
    blocks = neighbourhood.reshape(rim_count, neighbourhood.shape[1] // block_size, block_size)
    local_bubble = near_bubble - first_bubble
    sources = blocks[local_bubble, near_block]
    live_slot = jnp.arange(near_vals.shape[2])[None, None, :] < near_count[:, :, None]
    sources = jnp.where(live_slot[:, :, :, None], sources, jnp.zeros_like(sources))
    return jnp.einsum("brsij,brsj->bri", near_vals, sources, preferred_element_type=jnp.float32)


def far_kernel(centres, my_bubbles, reach):
    centre_mine = centres[:, my_bubbles]
    diff = centre_mine[:, :, None] - centres[:, None, :]
    direct_sq = jnp.sum(diff * diff, axis=0)
    mirrored = centre_mine[2][:, None] + centres[2][None, :]
    image_sq = diff[0] * diff[0] + diff[1] * diff[1] + mirrored * mirrored
    kernel = 1.0 / jnp.sqrt(direct_sq + 1.0) + 1.0 / jnp.sqrt(image_sq + 1.0)
    gap = jnp.abs(my_bubbles[:, None] - jnp.arange(centres.shape[1])[None, :])
    return jnp.where(gap > reach, kernel, jnp.zeros_like(kernel))


def per_device(
    density,
    right_side,
    inv_diag,
    near_vals,
    near_bubble,
    near_block,
    near_count,
    colour,
    moment_map,
    spread_map,
    centres,
):
    bub_dev = density.shape[0]
    panels_dev = density.shape[1]
    block_size = inv_diag.shape[2]
    my_index = lax.axis_index("bubble")
    my_bubbles = my_index * bub_dev + jnp.arange(bub_dev, dtype=jnp.int32)
    first_bubble = my_index * bub_dev - bub_dev
    kernel = far_kernel(centres, my_bubbles, bub_dev)
    relaxed = density
    for colour_now in range(2):
        dens_bf = relaxed.astype(jnp.bfloat16)
        panel_full = lax.all_gather(dens_bf, "panel", axis=1, tiled=True)
        neighbourhood = with_halo(panel_full, (("bubble", 0),), bub_dev)
        near = near_field(
            neighbourhood, near_vals, near_bubble, near_block, near_count, first_bubble, block_size
        )
        partial_value = jnp.einsum(
            "bki,bi->bk", moment_map, dens_bf, preferred_element_type=jnp.float32
        )
        own_moments = lax.psum(partial_value, "panel")
        all_moments = lax.all_gather(own_moments, "bubble", axis=0, tiled=True)
        far_coeff = jnp.dot(kernel, all_moments, precision=lax.Precision.HIGHEST).astype(
            jnp.bfloat16
        )
        far = jnp.einsum("bki,bk->bi", spread_map, far_coeff, preferred_element_type=jnp.float32)
        remainder = (right_side - near.reshape(bub_dev, panels_dev) - far).astype(jnp.bfloat16)
        remainder = remainder.reshape(bub_dev, panels_dev // block_size, block_size)
        updated = jnp.einsum(
            "brij,brj->bri", inv_diag, remainder, preferred_element_type=jnp.float32
        )
        relaxed = jnp.where(
            (colour == colour_now)[:, None], updated.reshape(bub_dev, panels_dev), relaxed
        )
    return relaxed


def solution(mesh):
    in_specs = (
        P("bubble", "panel"),
        P("bubble", "panel"),
        P("bubble", "panel", None, None),
        P("bubble", "panel", None, None, None),
        P("bubble", "panel", None),
        P("bubble", "panel", None),
        P("bubble", "panel"),
        P("bubble"),
        P("bubble", None, "panel"),
        P("bubble", None, "panel"),
        P(),
    )
    out_specs = P("bubble", "panel")
    return jax.shard_map(
        per_device, mesh=mesh, in_specs=in_specs, out_specs=out_specs, check_vma=False
    )
```

profile of v0, /device:TPU:0, one launch (start us, length us, event | category | flops | bytes accessed | tf_op | source)
XLA Modules:
  0.0 154.6 jit_solution(8585417838878019388)
XLA Ops:
  0.0 0.0 copy-start
  0.0 1.0 convert_element_type.18
  1.0 6.8 %all_gather.12 = bf16[8,12288]{1,0:T(8,128)(2,1)S(1)} all-gather(bf16[8,3072]{1,0:T(8,128)(2,1)S(1)} %convert_element_type.18), channel_id=1, replica_groups=mesh['bubble'=8,'panel'=4] {'panel'}, dimensions={1}, use_global_device_ids=true | all-gather | bytes 245760 | tf_op jit(solution)/shard_map/all_gather | solution.py:66
  7.8 3.6 %collective-permute-start = (bf16[8,12288]{1,0:T(8,128)(2,1)S(1)}, bf16[8,12288]{1,0:T(8,128)(2,1)S(1)}, u32[]{:S(2)}, u32[]{:S(2)}) collective-permute-start(bf16[8,12288]{1,0:T(8,128)(2,1)S(1)} %all_gather.12), channel_id=1, source_target_pairs={{0,4},{4,8},{8,12},{12,16},{16,20},{20,24},{24,28},{1,5},{5,9},{9,... | collective-permute-start | bytes 589832 | tf_op jit(solution)/shard_map/ppermute | solution.py:14
  11.4 1.3 collective-permute-start.1
  12.8 0.8 copy.18
  13.6 0.6 gather_fusion.1
  14.1 0.1 copy.19
  14.2 0.2 slice_reduce_fusion
  14.4 0.7 slice_bitcast_fusion
  15.1 0.9 convert_bitcast_fusion
  16.0 0.8 multiply_reduce_fusion
  16.7 1.5 fusion.16
  18.2 6.8 %psum.14 = f32[8,16]{1,0:T(8,128)S(1)} all-reduce(f32[8,16]{1,0:T(8,128)S(1)} %bitcast.107), channel_id=1, replica_groups=mesh['bubble'=8,'panel'=4] {'panel'}, use_global_device_ids=true, to_apply=%region_1.2 | all-reduce | flops 128 | bytes 1024 | tf_op jit(solution)/shard_map/psum | solution.py:74
  25.1 32.7 %all_gather.13 = f32[64,16]{1,0:T(8,128)S(1)} all-gather(f32[8,16]{1,0:T(8,128)S(1)} %psum.14), channel_id=1, replica_groups=mesh['bubble'=8,'panel'=4] {'bubble'}, dimensions={0}, use_global_device_ids=true | all-gather | bytes 4608 | tf_op jit(solution)/shard_map/all_gather | solution.py:75
  57.8 0.8 fusion.22
  58.6 0.1 copy.17
  58.7 0.1 reshape.62
  58.8 0.8 iota_compare_fusion
  59.6 0.1 fusion.32
  59.7 0.1 fusion
  59.8 0.0 copy-done
  59.8 0.3 fusion.35
  60.1 0.7 broadcast_compare_fusion.1
  60.7 0.0 collective-permute-done
  60.7 0.0 collective-permute-done.1
  60.8 0.1 copy.36
  60.9 4.4 %gather_fusion = bf16[768,128]{1,0:T(8,128)(2,1)S(1)} fusion(bf16[24,96,128]{2,1,0:T(8,128)(2,1)S(1)} %bitcast.101, s32[768]{0:T(1024)S(1)} %reshape.62), kind=kCustom, calls=%fused_computation | custom fusion | bytes 399360 | tf_op jit(solution)/shard_map/gather | solution.py:26
  65.3 0.3 select_bitcast_fusion.1
  65.6 0.0 copy-start.2
  65.6 11.6 %fusion.4 = f32[8,24,1,128,1]{3,2,4,1,0:T(1,128)S(1)} fusion(bf16[8,24,4,128,128]{4,3,2,1,0:T(8,128)(2,1)} %param.14, bf16[8,24,4,128,1]{3,2,1,0,4:T(4,128)(2,1)S(1)} %select_bitcast_fusion.1), kind=kOutput, calls=%fused_computation.11 | convolution fusion | flops 25165824 | bytes 25460736 | tf_op jit(solution)/shard_map/brsij,brsj->bri/dot_general | solution.py:29
  77.3 0.0 copy-done.2
  77.3 0.0 copy-start.1
  77.3 0.0 copy-start.3
  77.3 6.2 %fusion.14 = f32[8,24,1,128]{3,2,1,0:T(1,128)S(1)} fusion(bf16[8,24,128,128]{3,2,1,0:T(8,128)(2,1)} %param.13, bf16[8,24,128,1]{2,0,1,3:T(8,128)(2,1)S(1)} %fusion.18), kind=kOutput, calls=%fused_computation.27 | convolution fusion | flops 6291456 | bytes 6438912 | tf_op jit(solution)/shard_map/brij,brj->bri/dot_general | solution.py:82
  83.5 0.0 copy-done.1
  83.5 0.1 fusion.25
  83.6 5.6 %all_gather.14 = bf16[8,12288]{1,0:T(8,128)(2,1)S(1)} all-gather(bf16[8,3072]{1,0:T(8,128)(2,1)S(1)} %fusion.25), channel_id=1, replica_groups=mesh['bubble'=8,'panel'=4] {'panel'}, dimensions={1}, use_global_device_ids=true | all-gather | bytes 245760 | tf_op jit(solution)/shard_map/all_gather | solution.py:66
  89.2 2.5 %collective-permute-start.2 = (bf16[8,12288]{1,0:T(8,128)(2,1)S(1)}, bf16[8,12288]{1,0:T(8,128)(2,1)S(1)}, u32[]{:S(2)}, u32[]{:S(2)}) collective-permute-start(bf16[8,12288]{1,0:T(8,128)(2,1)S(1)} %all_gather.14), channel_id=1, source_target_pairs={{0,4},{4,8},{8,12},{12,16},{16,20},{20,24},{24,28},{1,5},{5,9},{9,... | collective-permute-start | bytes 589832 | tf_op jit(solution)/shard_map/ppermute | solution.py:14
  91.8 1.3 collective-permute-start.3
  93.1 0.0 copy-done.3
  93.1 0.4 fusion.12
  93.5 6.2 %psum.15 = f32[8,16]{1,0:T(8,128)S(1)} all-reduce(f32[8,16]{1,0:T(8,128)S(1)} %bitcast.108), channel_id=1, replica_groups=mesh['bubble'=8,'panel'=4] {'panel'}, use_global_device_ids=true, to_apply=%region_2.3 | all-reduce | flops 128 | bytes 1024 | tf_op jit(solution)/shard_map/psum | solution.py:74
  99.6 31.2 %all_gather.15 = f32[64,16]{1,0:T(8,128)S(1)} all-gather(f32[8,16]{1,0:T(8,128)S(1)} %psum.15), channel_id=1, replica_groups=mesh['bubble'=8,'panel'=4] {'bubble'}, dimensions={0}, use_global_device_ids=true | all-gather | bytes 4608 | tf_op jit(solution)/shard_map/all_gather | solution.py:75
  130.8 0.1 fusion.1
  130.9 0.3 fusion.33
  131.2 0.0 collective-permute-done.2
  131.2 0.0 collective-permute-done.3
  131.3 0.1 copy.37
  131.4 4.4 %gather_fusion.2 = bf16[768,128]{1,0:T(8,128)(2,1)S(1)} fusion(bf16[24,96,128]{2,1,0:T(8,128)(2,1)S(1)} %bitcast.100, s32[768]{0:T(1024)S(1)} %reshape.62), kind=kCustom, calls=%fused_computation.2 | custom fusion | bytes 399360 | tf_op jit(solution)/shard_map/gather | solution.py:26
  135.8 0.3 select_bitcast_fusion
  136.1 11.6 %fusion.2 = f32[8,24,1,128,1]{3,2,4,1,0:T(1,128)S(1)} fusion(bf16[8,24,4,128,128]{4,3,2,1,0:T(8,128)(2,1)} %param.14, bf16[8,24,4,128,1]{3,2,1,0,4:T(4,128)(2,1)S(1)} %select_bitcast_fusion), kind=kOutput, calls=%fused_computation.9 | convolution fusion | flops 25165824 | bytes 25460736 | tf_op jit(solution)/shard_map/brsij,brsj->bri/dot_general | solution.py:29
  147.7 6.1 %fusion.10 = f32[8,24,1,128]{3,2,1,0:T(1,128)S(1)} fusion(bf16[8,24,128,128]{3,2,1,0:T(8,128)(2,1)} %param.13, bf16[8,24,128,1]{2,0,1,3:T(8,128)(2,1)S(1)} %fusion.19), kind=kOutput, calls=%fused_computation.23 | convolution fusion | flops 6291456 | bytes 6438912 | tf_op jit(solution)/shard_map/brij,brj->bri/dot_general | solution.py:82
  153.8 0.8 bitcast_select_fusion
  (7 shorter events, 0.2 us)
Async XLA Ops:
  0.0 59.8 %copy-start = (bf16[8,16,3072]{2,1,0:T(8,128)(2,1)S(1)}, bf16[8,16,3072]{2,1,0:T(8,128)(2,1)}, u32[]{:S(2)}) copy-start(bf16[8,16,3072]{2,1,0:T(8,128)(2,1)} %param.20) | copy-start | bytes 2359300
  7.8 52.9 %collective-permute-start = (bf16[8,12288]{1,0:T(8,128)(2,1)S(1)}, bf16[8,12288]{1,0:T(8,128)(2,1)S(1)}, u32[]{:S(2)}, u32[]{:S(2)}) collective-permute-start(bf16[8,12288]{1,0:T(8,128)(2,1)S(1)} %all_gather.12), channel_id=1, source_target_pairs={{0,4},{4,8},{8,12},{12,16},{16,20},{20,24},{24,28},{1,5},{5,9},{9,... | collective-permute-start | bytes 589832 | tf_op jit(solution)/shard_map/ppermute | solution.py:14
  11.4 49.3 %collective-permute-start.1 = (bf16[8,12288]{1,0:T(8,128)(2,1)S(1)}, bf16[8,12288]{1,0:T(8,128)(2,1)S(1)}, u32[]{:S(2)}, u32[]{:S(2)}) collective-permute-start(bf16[8,12288]{1,0:T(8,128)(2,1)S(1)} %all_gather.12), channel_id=1, source_target_pairs={{4,0},{8,4},{12,8},{16,12},{20,16},{24,20},{28,24},{5,1},{9,5},{13... | collective-permute-start | bytes 589832 | tf_op jit(solution)/shard_map/ppermute | solution.py:15
  65.6 11.7 %copy-start.2 = (f32[8,3072]{1,0:T(8,128)S(1)}, f32[8,3072]{1,0:T(8,128)}, u32[]{:S(2)}) copy-start(f32[8,3072]{1,0:T(8,128)} %param.12) | copy-start | bytes 294916
  77.3 6.2 %copy-start.1 = (f32[8,3072]{1,0:T(8,128)S(1)}, f32[8,3072]{1,0:T(8,128)}, u32[]{:S(2)}) copy-start(f32[8,3072]{1,0:T(8,128)} %param.11) | copy-start | bytes 294916
  77.3 15.8 %copy-start.3 = (bf16[8,16,3072]{2,1,0:T(8,128)(2,1)S(1)}, bf16[8,16,3072]{2,1,0:T(8,128)(2,1)}, u32[]{:S(2)}) copy-start(bf16[8,16,3072]{2,1,0:T(8,128)(2,1)} %param.19) | copy-start | bytes 2359300
  89.2 42.0 %collective-permute-start.2 = (bf16[8,12288]{1,0:T(8,128)(2,1)S(1)}, bf16[8,12288]{1,0:T(8,128)(2,1)S(1)}, u32[]{:S(2)}, u32[]{:S(2)}) collective-permute-start(bf16[8,12288]{1,0:T(8,128)(2,1)S(1)} %all_gather.14), channel_id=1, source_target_pairs={{0,4},{4,8},{8,12},{12,16},{16,20},{20,24},{24,28},{1,5},{5,9},{9,... | collective-permute-start | bytes 589832 | tf_op jit(solution)/shard_map/ppermute | solution.py:14
  91.8 39.5 %collective-permute-start.3 = (bf16[8,12288]{1,0:T(8,128)(2,1)S(1)}, bf16[8,12288]{1,0:T(8,128)(2,1)S(1)}, u32[]{:S(2)}, u32[]{:S(2)}) collective-permute-start(bf16[8,12288]{1,0:T(8,128)(2,1)S(1)} %all_gather.14), channel_id=1, source_target_pairs={{4,0},{8,4},{12,8},{16,12},{20,16},{24,20},{28,24},{5,1},{9,5},{13... | collective-permute-start | bytes 589832 | tf_op jit(solution)/shard_map/ppermute | solution.py:15
where the time goes:
time: 155 us
  blocking collectives  89.3 us (58%)
  matrix products  38.2 us (25%)
  local copies, waits for them, and re-layouts  11.6 us (7%)
  starting transfers between devices  8.75 us (6%)
  other arithmetic  6.48 us (4%)
    all_gather x2, blocking collectives, per_device(): all_moments = lax.all_gather(own_moments, 'bubble', axis=0, tiled=True)  63.9 us
    dot_general x2, matrix products, near_field(): jnp.einsum('brsij,brsj->bri', near_vals, sources, preferred_element_type=...  23.2 us
    psum x2, blocking collectives, per_device(): own_moments = lax.psum(partial_value, 'panel')  13 us
    all_gather x2, blocking collectives, per_device(): panel_full = lax.all_gather(dens_bf, 'panel', axis=1, tiled=True)  12.4 us
    dot_general x2, matrix products, per_device(): jnp.einsum('brij,brj->bri', inv_diag, remainder, preferred_element_type=j...  12.3 us
    gather x2, local copies, waits for them, and re-layouts, near_field(): sources = blocks[local_bubble, near_block]  8.86 us
    ppermute x2, starting transfers between devices, with_halo(): before = lax.ppermute(last, axis, up)  6.17 us
  transfers between devices with their start and end apart: 4, of which 0 were waited for; matrix products, arithmetic and copies ran while one was open for 6% of the time, Pallas kernels for 0%

commit v1 on v0

v1 whole, which is shorter than its diff:
```python
import functools

import jax
import jax.numpy as jnp
from jax import lax
from jax.experimental import pallas as pl
from jax.experimental.pallas import tpu as pltpu
from jax.sharding import PartitionSpec as P

MESH = pl.DeviceIdType.MESH
F32 = jnp.float32
BF16 = jnp.bfloat16


def dot_nt(left, right):
    return lax.dot_general(left, right, (((1,), (1,)), ((), ())), preferred_element_type=F32)


def kernel(
    nbub,
    npan,
    groups,
    dens_ref,
    rhs_ref,
    inv_hbm,
    near_hbm,
    src_bubble_ref,
    src_block_ref,
    count_ref,
    colour_ref,
    mom_hbm,
    spread_hbm,
    centres_ref,
    out_ref,
    near_v,
    inv_v,
    mom_v,
    spread_v,
    hood,
    onehot,
    picked,
    part_mom,
    all_mom,
    green,
    far_v,
    near_sem,
    inv_sem,
    map_sem,
    dens_send,
    dens_recv,
    part_send,
    part_recv,
    mom_send,
    mom_recv,
):
    bub, panels = dens_ref.shape
    rows, slots, blk = near_v.shape[1], near_v.shape[2], near_v.shape[3]
    pairs = rows // 2
    chunk = rows * bub
    moments = mom_v.shape[0] // bub
    lanes = bub * moments
    peers = 3 * npan
    group_pairs = pairs // groups
    me_b, me_p = lax.axis_index("bubble"), lax.axis_index("panel")
    own_slot = npan + me_p

    def rows_of(slot, first, size):
        return pl.ds(pl.multiple_of(slot * chunk + first, 16), size)

    def cols(first, size):
        return pl.ds(pl.multiple_of(first, 128), size)

    def for_peers(do):
        def step(j, carry):
            side, p = j // npan, lax.rem(j, npan)
            other = me_b + side - 1
            ok = (other >= 0) & (other < nbub) & jnp.logical_not((side == 1) & (p == me_p))

            @pl.when(ok)
            def _():
                do(j, side, p, other)

            return carry

        lax.fori_loop(0, peers, step, 0)

    def for_others(count, me, do):
        def step(j, carry):
            @pl.when(j != me)
            def _():
                do(j)

            return carry

        lax.fori_loop(0, count, step, 0)

    barrier = pltpu.get_barrier_semaphore()

    def greet(j, side, p, other):
        pl.semaphore_signal(barrier, inc=1, device_id=(other, p), device_id_type=MESH)

    def greet_bubble(j):
        pl.semaphore_signal(barrier, inc=1, device_id=(j, me_p), device_id_type=MESH)

    for_peers(greet)
    for_others(nbub, me_b, greet_bubble)

    mom_copy = pltpu.make_async_copy(mom_hbm, mom_v, map_sem.at[0])
    spread_copy = pltpu.make_async_copy(spread_hbm, spread_v, map_sem.at[1])
    mom_copy.start()

    def near_copy(q):
        two = pl.ds(2 * q, 2)
        return pltpu.make_async_copy(near_hbm.at[:, two], near_v.at[:, two], near_sem.at[q])

    def inv_copy(q):
        two = pl.ds(2 * q, 2)
        return pltpu.make_async_copy(inv_hbm.at[:, two], inv_v.at[:, two], inv_sem.at[q])

    def start_load(q, carry):
        near_copy(q).start()
        inv_copy(q).start()
        return carry

    lax.fori_loop(0, 1, start_load, 0)
    spread_copy.start()
    lax.fori_loop(1, pairs, start_load, 0)

    def place(q, carry):
        both = jnp.concatenate(
            [dens_ref[:, cols(2 * q * blk, blk)], dens_ref[:, cols((2 * q + 1) * blk, blk)]], axis=0
        )
        hood[0, rows_of(own_slot, q * 16, 16), :] = both.astype(BF16)
        return carry

    lax.fori_loop(0, pairs, place, 0)

    @pl.when(me_b == 0)
    def _():
        hood[:, pl.ds(0, npan * chunk), :] = jnp.zeros((2, npan * chunk, blk), BF16)

    @pl.when(me_b == nbub - 1)
    def _():
        hood[:, pl.ds(2 * npan * chunk, npan * chunk), :] = jnp.zeros((2, npan * chunk, blk), BF16)

    sides = (me_b > 0).astype(jnp.int32) + (me_b < nbub - 1).astype(jnp.int32)
    pl.semaphore_wait(barrier, npan - 1 + npan * sides + nbub - 1)

    def dens_copy(sem, phase, first, size, j, side, p, other):
        piece = hood.at[phase, rows_of(own_slot, first, size)]
        back = (2 - side) * npan + me_p
        return pltpu.make_async_remote_copy(
            src_ref=piece,
            dst_ref=hood.at[phase, rows_of(back, first, size)],
            send_sem=dens_send.at[sem, j],
            recv_sem=dens_recv.at[sem, back],
            device_id=(other, p),
            device_id_type=MESH,
        )

    def dens_arrival(sem, phase, first, size, j, side, p, other):
        piece = hood.at[phase, rows_of(j, first, size)]
        return pltpu.make_async_remote_copy(
            src_ref=piece,
            dst_ref=piece,
            send_sem=dens_send.at[sem, j],
            recv_sem=dens_recv.at[sem, j],
            device_id=(other, p),
            device_id_type=MESH,
        )

    def part_copy(phase, slot, p):
        return pltpu.make_async_remote_copy(
            src_ref=part_mom.at[phase, me_p],
            dst_ref=part_mom.at[phase, slot],
            send_sem=part_send.at[phase, p],
            recv_sem=part_recv.at[phase, slot],
            device_id=(me_b, p),
            device_id_type=MESH,
        )

    def mom_copy_to(phase, slot, b):
        return pltpu.make_async_remote_copy(
            src_ref=all_mom.at[phase, me_b],
            dst_ref=all_mom.at[phase, slot],
            send_sem=mom_send.at[phase, b],
            recv_sem=mom_recv.at[phase, slot],
            device_id=(b, me_p),
            device_id_type=MESH,
        )

    group_rows = group_pairs * 16
    pieces = [(0, 0, 0, chunk)] + [(1 + g, 1, g * group_rows, group_rows) for g in range(groups)]

    for_peers(lambda *a: dens_copy(*pieces[0], *a).start())

    lane = lax.broadcasted_iota(jnp.int32, (bub, lanes), 1)
    row = lax.broadcasted_iota(jnp.int32, (bub, lanes), 0)
    diagonal = lane // moments == row

    def send_moments(phase, source):
        partial = jnp.where(diagonal, dot_nt(source[...].astype(BF16), mom_v[...]), 0.0)
        total = jnp.sum(partial, axis=0, keepdims=True)
        part_mom[phase, me_p] = jnp.broadcast_to(total, (bub, lanes))
        for_others(npan, me_p, lambda p: part_copy(phase, me_p, p).start())

    def pass_moments(phase):
        for_others(npan, me_p, lambda p: part_copy(phase, p, p).wait_recv())
        total = part_mom[phase, 0]
        for p in range(1, npan):
            total = total + part_mom[phase, p]
        all_mom[phase, me_b] = total
        for_others(nbub, me_b, lambda b: mom_copy_to(phase, me_b, b).start())

    def far_field(phase):
        for_others(nbub, me_b, lambda b: mom_copy_to(phase, b, b).wait_recv())
        total = green[0] * all_mom[phase, 0]
        for b in range(1, nbub):
            total = total + green[b] * all_mom[phase, b]
        shift = moments
        while shift < lanes:
            total = total + pltpu.roll(total, shift, 1)
            shift *= 2
        coeff = jnp.where(diagonal, total, 0.0).astype(BF16)
        far_v[...] = jnp.dot(coeff, spread_v[...], preferred_element_type=F32)

    mom_copy.wait()
    send_moments(0, dens_ref)

    def build(b, carry):
        counts = jnp.broadcast_to(count_ref[pl.ds(b, 1), :], (rows, rows))
        on = lax.broadcasted_iota(jnp.int32, (rows, rows), 0) == lax.broadcasted_iota(
            jnp.int32, (rows, rows), 1
        )
        live = jnp.sum(jnp.where(on, counts.astype(F32), 0.0), axis=1, keepdims=True)
        near_bub = src_bubble_ref[b] - (me_b * bub - bub)
        block = src_block_ref[b]
        index = (near_bub // bub * npan + block // rows) * chunk
        index = index + lax.rem(block, rows) * bub + lax.rem(near_bub, bub)
        slot = lax.broadcasted_iota(jnp.int32, (rows, slots), 1).astype(F32)
        index = jnp.where(slot < live, index, -1)
        wide = jnp.concatenate([index[:, s : s + 1] for s in range(slots)], axis=0)
        wide = jnp.broadcast_to(wide, (slots * rows, 128))
        place_of = lax.broadcasted_iota(jnp.int32, (slots * rows, 128), 1)
        for c in range(peers * chunk // 128):
            hit = wide == place_of + c * 128
            onehot[b, :, c * 128 : (c + 1) * 128] = jnp.where(hit, 1.0, 0.0).astype(BF16)
        return carry

    lax.fori_loop(0, bub, build, 0)

    which = lax.broadcasted_iota(jnp.int32, (bub, nbub * bub), 1)
    mine = which == me_b * bub + lax.broadcasted_iota(jnp.int32, (bub, nbub * bub), 0)
    own = [
        jnp.sum(jnp.where(mine, centres_ref[c : c + 1, :], 0.0), axis=1, keepdims=True)
        for c in range(3)
    ]
    spot = lax.broadcasted_iota(jnp.int32, (nbub * bub, lanes), 0)
    over = lax.broadcasted_iota(jnp.int32, (nbub * bub, lanes), 1) // moments
    for b in range(nbub):
        spread_out = jnp.where(spot == over + b * bub, 1.0, 0.0)
        wide = jnp.dot(
            centres_ref[...], spread_out, precision=lax.Precision.HIGHEST, preferred_element_type=F32
        )
        dx, dy, dz = [own[c] - wide[c : c + 1, :] for c in range(3)]
        flat = dx * dx + dy * dy
        up = own[2] + wide[2:3, :]
        value = 1.0 / jnp.sqrt(flat + dz * dz + 1.0) + 1.0 / jnp.sqrt(flat + up * up + 1.0)
        gap = jnp.abs(me_b * bub + row - (b * bub + lane // moments))
        green[b] = jnp.where(gap > bub, value, 0.0)

    tint = jnp.zeros((bub, blk), jnp.int32)
    line = lax.broadcasted_iota(jnp.int32, (bub, blk), 0)
    for b in range(bub):
        tint = jnp.where(line == b, colour_ref[b], tint)

    pass_moments(0)

    def pick(phase):
        def step(b, carry):
            got = jnp.dot(onehot[b], hood[phase], preferred_element_type=F32)
            picked[pl.ds(b, slots * rows, stride=bub), :] = got
            return carry

        lax.fori_loop(0, bub, step, 0)

    def by_bubble(left, right_of):
        even = jnp.zeros((bub, blk), F32)
        odd = jnp.zeros((bub, blk), F32)
        for b in range(bub):
            got = dot_nt(left, right_of(b))
            even = jnp.where(line == b, got[:bub, :blk], even)
            odd = jnp.where(line == b, got[bub:, blk:], odd)
        return jnp.concatenate([even, odd], axis=0)

    def stacked(ref, q):
        first, second = cols(2 * q * blk, blk), cols((2 * q + 1) * blk, blk)
        return jnp.concatenate([ref[:, first], ref[:, second]], axis=0)

    def near_block(b, q):
        return jnp.concatenate(
            [
                jnp.concatenate([near_v[b, 2 * q + o, s] for s in range(slots)], axis=1)
                for o in range(2)
            ],
            axis=0,
        )

    def inv_block(b, q):
        return jnp.concatenate([inv_v[b, 2 * q], inv_v[b, 2 * q + 1]], axis=0)

    def solve(phase, old_ref, q):
        left = jnp.concatenate(
            [
                picked[pl.ds(pl.multiple_of((s * rows + 2 * q) * bub, 16), 16), :].astype(BF16)
                for s in range(slots)
            ],
            axis=1,
        )
        near = by_bubble(left, lambda b: near_block(b, q))
        rest = (stacked(rhs_ref, q) - near - stacked(far_v, q)).astype(BF16)
        updated = by_bubble(rest, lambda b: inv_block(b, q))
        both = jnp.concatenate([tint, tint], axis=0)
        new = jnp.where(both == phase, updated, stacked(old_ref, q))
        out_ref[:, cols(2 * q * blk, blk)] = new[:bub]
        out_ref[:, cols((2 * q + 1) * blk, blk)] = new[bub:]
        return new

    spread_copy.wait()
    far_field(0)
    for_peers(lambda *a: dens_arrival(*pieces[0], *a).wait_recv())
    pick(0)

    def first_colour(q, carry):
        near_copy(q).wait()
        inv_copy(q).wait()
        new = solve(0, dens_ref, q)
        hood[1, rows_of(own_slot, q * 16, 16), :] = new.astype(BF16)
        return carry

    for g in range(groups):
        lax.fori_loop(g * group_pairs, (g + 1) * group_pairs, first_colour, 0)
        for_peers(lambda *a: dens_copy(*pieces[1 + g], *a).start())

    send_moments(1, out_ref)
    pass_moments(1)
    far_field(1)
    for g in range(groups):
        for_peers(lambda *a: dens_arrival(*pieces[1 + g], *a).wait_recv())
    pick(1)

    def second_colour(q, carry):
        solve(1, out_ref, q)
        return carry

    lax.fori_loop(0, pairs, second_colour, 0)

    for piece in pieces:
        for_peers(lambda *a: dens_copy(*piece, *a).wait_send())
    for phase in range(2):
        for_others(npan, me_p, lambda p: part_copy(phase, me_p, p).wait_send())
        for_others(nbub, me_b, lambda b: mom_copy_to(phase, me_b, b).wait_send())


def per_device(
    density,
    right_side,
    inv_diag,
    near_vals,
    near_bubble,
    near_block,
    near_count,
    colour,
    moment_map,
    spread_map,
    centres,
):
    nbub, npan = lax.axis_size("bubble"), lax.axis_size("panel")
    bub, panels = density.shape
    rows, slots, blk = near_vals.shape[1:4]
    moments = moment_map.shape[1]
    lanes = bub * moments
    groups = 3 if (rows // 2) % 3 == 0 else 1
    pairs = rows // 2
    chunk = rows * bub
    hood_rows = 3 * npan * chunk
    vmem = pl.BlockSpec(memory_space=pltpu.VMEM)
    smem = pl.BlockSpec(memory_space=pltpu.SMEM)
    hbm = pl.BlockSpec(memory_space=pl.ANY)
    dma = pltpu.SemaphoreType.DMA
    return pl.pallas_call(
        functools.partial(kernel, nbub, npan, groups),
        out_shape=jax.ShapeDtypeStruct(density.shape, F32),
        in_specs=[vmem, vmem, hbm, hbm, vmem, vmem, vmem, smem, hbm, hbm, vmem],
        out_specs=vmem,
        scratch_shapes=[
            pltpu.VMEM(near_vals.shape, BF16),
            pltpu.VMEM(inv_diag.shape, BF16),
            pltpu.VMEM((lanes, panels), BF16),
            pltpu.VMEM((lanes, panels), BF16),
            pltpu.VMEM((2, hood_rows, blk), BF16),
            pltpu.VMEM((bub, slots * rows, hood_rows), BF16),
            pltpu.VMEM((slots * rows * bub, blk), F32),
            pltpu.VMEM((2, npan, bub, lanes), F32),
            pltpu.VMEM((2, nbub, bub, lanes), F32),
            pltpu.VMEM((nbub, bub, lanes), F32),
            pltpu.VMEM((bub, panels), F32),
            dma((pairs,)),
            dma((pairs,)),
            dma((2,)),
            dma((1 + groups, 3 * npan)),
            dma((1 + groups, 3 * npan)),
            dma((2, npan)),
            dma((2, npan)),
            dma((2, nbub)),
            dma((2, nbub)),
        ],
        compiler_params=pltpu.CompilerParams(
            collective_id=0, has_side_effects=True, vmem_limit_bytes=56 * 1024 * 1024
        ),
    )(
        density,
        right_side,
        inv_diag,
        near_vals,
        near_bubble,
        near_block,
        near_count,
        colour,
        moment_map.reshape(lanes, panels),
        spread_map.reshape(lanes, panels),
        centres,
    )


def solution(mesh):
    in_specs = (
        P("bubble", "panel"),
        P("bubble", "panel"),
        P("bubble", "panel", None, None),
        P("bubble", "panel", None, None, None),
        P("bubble", "panel", None),
        P("bubble", "panel", None),
        P("bubble", "panel"),
        P("bubble"),
        P("bubble", None, "panel"),
        P("bubble", None, "panel"),
        P(),
    )
    out_specs = P("bubble", "panel")
    return jax.shard_map(
        per_device, mesh=mesh, in_specs=in_specs, out_specs=out_specs, check_vma=False
    )
```

time: 155 us -> 63.4 us (0.41)
  blocking collectives: 89.3 us -> 0 us
  Pallas kernels: 0 us -> 58.6 us
  matrix products: 38.2 us -> 0 us
  starting transfers between devices: 8.75 us -> 0 us
  local copies, waits for them, and re-layouts: 11.6 us -> 4.47 us
  other arithmetic: 6.48 us -> 0 us
    all_gather x4 -> x0, blocking collectives: 76.3 us -> none  [the longest x2 63.9 us: per_device(): all_moments = lax.all_gather(own_moments, 'bubble', axis=0, tiled=True)]
    pallas_call x0 -> x1, Pallas kernels: none -> 58.6 us  [per_device(): pl.pallas_call(functools.partial(kernel, nbub, npan, groups), out_shape=j...]
    dot_general x10 -> x0, matrix products: 38.2 us -> none  [the longest x2 23.2 us: near_field(): jnp.einsum('brsij,brsj->bri', near_vals, sources, preferred_element_type=...]
    psum x2 -> x0, blocking collectives: 13 us -> none  [per_device(): own_moments = lax.psum(partial_value, 'panel')]
    gather x4 -> x0, local copies, waits for them, and re-layouts: 9.49 us -> none  [the longest x2 8.86 us: near_field(): sources = blocks[local_bubble, near_block]]
    ppermute x4 -> x0, starting transfers between devices: 8.75 us -> none  [the longest x2 6.17 us: with_halo(): before = lax.ppermute(last, axis, up)]
    unnamed x11 -> x3, local copies, waits for them, and re-layouts: 0.97 us -> 4.47 us
    convert_element_type x3 -> x0, other arithmetic: 1.97 us -> none  [per_device(): dens_bf = relaxed.astype(jnp.bfloat16)]
  transfers between devices with their start and end apart: 4 -> 0, of which waited for: 0 -> 0; matrix products, arithmetic and copies ran while one was open for 6% -> 0% of each run, Pallas kernels for 0% -> 0%
where the time goes in v1:
time: 63.4 us; the launch traced here: 63 us
  Pallas kernels  58.6 us (92%)
  local copies, waits for them, and re-layouts  4.47 us (7%)
    pallas_call x1, Pallas kernels, per_device(): pl.pallas_call(functools.partial(kernel, nbub, npan, groups), out_shape=j...  58.6 us
    unnamed x3, local copies, waits for them, and re-layouts  4.47 us

profile of v1, /device:TPU:0, one launch (start us, length us, event | category | flops | bytes accessed | tf_op | source)
XLA Modules:
  0.0 63.0 jit_solution(5566298047788084208)
XLA Ops:
  0.0 1.5 %copy.12.src_bubble_ref = s32[8,24,4]{2,1,0:T(8,128)} copy(s32[8,24,4]{1,2,0:T(4,128)} %param.15) | data formatting | bytes 6144 | tf_op args[4]
  1.5 1.5 %copy.13.src_block_ref = s32[8,24,4]{2,1,0:T(8,128)} copy(s32[8,24,4]{1,2,0:T(4,128)} %param.16) | data formatting | bytes 6144 | tf_op args[5]
  2.9 58.6 %shard_map.109 = f32[8,3072]{1,0:T(8,128)} custom-call(f32[8,3072]{1,0:T(8,128)} %dens_ref.1, f32[8,3072]{1,0:T(8,128)} %rhs_ref.1, bf16[8,24,128,128]{3,2,1,0:T(8,128)(2,1)} %inv_hbm.1, bf16[8,24,4,128,128]{4,3,2,1,0:T(8,128)(2,1)} %near_hbm.1, s32[8,24,4]{2,1,0:T(8,128)} %copy.12.src_bubble_ref, s32[8,24,4]{2,1,0:T(8,128)} %copy.13.src_block_ref, ...), custom_call_target="tpu_custom_call" | custom-call | tf_op jit(solution)/shard_map/pallas_call | solution.py:391
  61.5 1.5 %copy.15 = f32[8,3072]{1,0:T(8,128)} copy(f32[8,3072]{1,0:T(8,128)} %shard_map.109) | data formatting | bytes 196608

commit v2 on v1

--- a/solution.py
+++ b/solution.py
@@ -228,23 +228,32 @@
     send_moments(0, dens_ref)
 
     def build(b, carry):
-        counts = jnp.broadcast_to(count_ref[pl.ds(b, 1), :], (rows, rows))
         on = lax.broadcasted_iota(jnp.int32, (rows, rows), 0) == lax.broadcasted_iota(
             jnp.int32, (rows, rows), 1
         )
-        live = jnp.sum(jnp.where(on, counts.astype(F32), 0.0), axis=1, keepdims=True)
         near_bub = src_bubble_ref[b] - (me_b * bub - bub)
         block = src_block_ref[b]
         index = (near_bub // bub * npan + block // rows) * chunk
         index = index + lax.rem(block, rows) * bub + lax.rem(near_bub, bub)
-        slot = lax.broadcasted_iota(jnp.int32, (rows, slots), 1).astype(F32)
-        index = jnp.where(slot < live, index, -1)
-        wide = jnp.concatenate([index[:, s : s + 1] for s in range(slots)], axis=0)
+        slot = lax.broadcasted_iota(jnp.int32, (slots, rows), 0)
+        index = jnp.where(slot < count_ref[pl.ds(b, 1), :], index, -1).astype(F32)
+        wide = jnp.concatenate(
+            [
+                jnp.sum(
+                    jnp.where(on, jnp.broadcast_to(index[s : s + 1, :], (rows, rows)), 0.0),
+                    axis=1,
+                    keepdims=True,
+                )
+                for s in range(slots)
+            ],
+            axis=0,
+        )
         wide = jnp.broadcast_to(wide, (slots * rows, 128))
-        place_of = lax.broadcasted_iota(jnp.int32, (slots * rows, 128), 1)
+        place_of = lax.broadcasted_iota(jnp.int32, (slots * rows, 128), 1).astype(F32)
+        mine_rows = pl.ds(pl.multiple_of(b * slots * rows, 16), slots * rows)
         for c in range(peers * chunk // 128):
-            hit = wide == place_of + c * 128
-            onehot[b, :, c * 128 : (c + 1) * 128] = jnp.where(hit, 1.0, 0.0).astype(BF16)
+            hit = wide == place_of + float(c * 128)
+            onehot[mine_rows, c * 128 : (c + 1) * 128] = jnp.where(hit, 1.0, 0.0).astype(BF16)
         return carry
 
     lax.fori_loop(0, bub, build, 0)
@@ -277,12 +286,17 @@
     pass_moments(0)
 
     def pick(phase):
-        def step(b, carry):
-            got = jnp.dot(onehot[b], hood[phase], preferred_element_type=F32)
-            picked[pl.ds(b, slots * rows, stride=bub), :] = got
+        size = slots * rows
+        half = bub // 2
+
+        def step(h, carry):
+            some = onehot[pl.ds(pl.multiple_of(h * half * size, 16), half * size), :]
+            got = jnp.dot(some, hood[phase], preferred_element_type=F32)
+            for o in range(half):
+                picked[pl.ds(h * half + o, size, stride=bub), :] = got[o * size : (o + 1) * size]
             return carry
 
-        lax.fori_loop(0, bub, step, 0)
+        lax.fori_loop(0, 2, step, 0)
 
     def by_bubble(left, right_of):
         even = jnp.zeros((bub, blk), F32)
@@ -309,51 +323,61 @@
     def inv_block(b, q):
         return jnp.concatenate([inv_v[b, 2 * q], inv_v[b, 2 * q + 1]], axis=0)
 
-    def solve(phase, old_ref, q):
-        left = jnp.concatenate(
-            [
-                picked[pl.ds(pl.multiple_of((s * rows + 2 * q) * bub, 16), 16), :].astype(BF16)
-                for s in range(slots)
-            ],
-            axis=1,
-        )
-        near = by_bubble(left, lambda b: near_block(b, q))
-        rest = (stacked(rhs_ref, q) - near - stacked(far_v, q)).astype(BF16)
-        updated = by_bubble(rest, lambda b: inv_block(b, q))
-        both = jnp.concatenate([tint, tint], axis=0)
-        new = jnp.where(both == phase, updated, stacked(old_ref, q))
-        out_ref[:, cols(2 * q * blk, blk)] = new[:bub]
-        out_ref[:, cols((2 * q + 1) * blk, blk)] = new[bub:]
-        return new
+    both_tint = jnp.concatenate([tint, tint], axis=0)
+
+    def solve(phase, old_ref, some):
+        rests = []
+        for q in some:
+            left = jnp.concatenate(
+                [
+                    picked[pl.ds(pl.multiple_of((s * rows + 2 * q) * bub, 16), 16), :].astype(BF16)
+                    for s in range(slots)
+                ],
+                axis=1,
+            )
+            near = by_bubble(left, lambda b: near_block(b, q))
+            rests.append((stacked(rhs_ref, q) - near - stacked(far_v, q)).astype(BF16))
+        news = []
+        for q, rest in zip(some, rests):
+            updated = by_bubble(rest, lambda b: inv_block(b, q))
+            news.append(jnp.where(both_tint == phase, updated, stacked(old_ref, q)))
+        for q, new in zip(some, news):
+            out_ref[:, cols(2 * q * blk, blk)] = new[:bub]
+            out_ref[:, cols((2 * q + 1) * blk, blk)] = new[bub:]
+        return news
 
     spread_copy.wait()
-    far_field(0)
     for_peers(lambda *a: dens_arrival(*pieces[0], *a).wait_recv())
     pick(0)
-
-    def first_colour(q, carry):
-        near_copy(q).wait()
-        inv_copy(q).wait()
-        new = solve(0, dens_ref, q)
-        hood[1, rows_of(own_slot, q * 16, 16), :] = new.astype(BF16)
+    far_field(0)
+    batch = 2 if group_pairs % 2 == 0 else 1
+
+    def first_colour(t, carry):
+        some = [batch * t + o for o in range(batch)]
+        for q in some:
+            near_copy(q).wait()
+            inv_copy(q).wait()
+        for q, new in zip(some, solve(0, dens_ref, some)):
+            hood[1, rows_of(own_slot, q * 16, 16), :] = new.astype(BF16)
         return carry
 
+    steps = group_pairs // batch
     for g in range(groups):
-        lax.fori_loop(g * group_pairs, (g + 1) * group_pairs, first_colour, 0)
+        lax.fori_loop(g * steps, (g + 1) * steps, first_colour, 0)
         for_peers(lambda *a: dens_copy(*pieces[1 + g], *a).start())
 
     send_moments(1, out_ref)
     pass_moments(1)
-    far_field(1)
     for g in range(groups):
         for_peers(lambda *a: dens_arrival(*pieces[1 + g], *a).wait_recv())
     pick(1)
-
-    def second_colour(q, carry):
-        solve(1, out_ref, q)
+    far_field(1)
+
+    def second_colour(t, carry):
+        solve(1, out_ref, [batch * t + o for o in range(batch)])
         return carry
 
-    lax.fori_loop(0, pairs, second_colour, 0)
+    lax.fori_loop(0, pairs // batch, second_colour, 0)
 
     for piece in pieces:
         for_peers(lambda *a: dens_copy(*piece, *a).wait_send())
@@ -399,7 +423,7 @@
             pltpu.VMEM((lanes, panels), BF16),
             pltpu.VMEM((lanes, panels), BF16),
             pltpu.VMEM((2, hood_rows, blk), BF16),
-            pltpu.VMEM((bub, slots * rows, hood_rows), BF16),
+            pltpu.VMEM((bub * slots * rows, hood_rows), BF16),
             pltpu.VMEM((slots * rows * bub, blk), F32),
             pltpu.VMEM((2, npan, bub, lanes), F32),
             pltpu.VMEM((2, nbub, bub, lanes), F32),
@@ -423,8 +447,8 @@
         right_side,
         inv_diag,
         near_vals,
-        near_bubble,
-        near_block,
+        near_bubble.transpose(0, 2, 1),
+        near_block.transpose(0, 2, 1),
         near_count,
         colour,
         moment_map.reshape(lanes, panels),

time: 63.4 us -> 51.6 us (0.81)
  Pallas kernels: 58.6 us -> 49.9 us
  local copies, waits for them, and re-layouts: 4.47 us -> 1.54 us
    pallas_call x1, Pallas kernels: 58.6 us -> 49.9 us  [per_device(): pl.pallas_call(functools.partial(kernel, nbub, npan, groups), out_shape=j...]
    unnamed x3 -> x1, local copies, waits for them, and re-layouts: 4.47 us -> 1.54 us
where the time goes in v2:
time: 51.6 us; the launch traced here: 51.4 us
  Pallas kernels  49.9 us (97%)
  local copies, waits for them, and re-layouts  1.54 us (3%)
    pallas_call x1, Pallas kernels, per_device(): pl.pallas_call(functools.partial(kernel, nbub, npan, groups), out_shape=j...  49.9 us
    unnamed x1, local copies, waits for them, and re-layouts  1.54 us

profile of v2, /device:TPU:0, one launch (start us, length us, event | category | flops | bytes accessed | tf_op | source)
XLA Modules:
  0.0 51.4 jit_solution(6464854174090495496)
XLA Ops:
  0.0 49.9 %shard_map.109 = f32[8,3072]{1,0:T(8,128)} custom-call(f32[8,3072]{1,0:T(8,128)} %dens_ref.1, f32[8,3072]{1,0:T(8,128)} %rhs_ref.1, bf16[8,24,128,128]{3,2,1,0:T(8,128)(2,1)} %inv_hbm.1, bf16[8,24,4,128,128]{4,3,2,1,0:T(8,128)(2,1)} %near_hbm.1, s32[8,4,24]{2,1,0:T(4,128)} %bitcast.6, s32[8,4,24]{2,1,0:T(4,128)} %bitcast.7, s32[8,24]{1,0:T(8,128)} %count_ref.1, ...), custom_call_target="tpu_custom_call" | custom-call | tf_op jit(solution)/shard_map/pallas_call | solution.py:415
  49.9 1.5 %copy.13 = f32[8,3072]{1,0:T(8,128)} copy(f32[8,3072]{1,0:T(8,128)} %shard_map.109) | data formatting | bytes 196608

commit v3 on v2

--- a/solution.py
+++ b/solution.py
@@ -298,72 +298,82 @@
 
         lax.fori_loop(0, 2, step, 0)
 
-    def by_bubble(left, right_of):
-        even = jnp.zeros((bub, blk), F32)
-        odd = jnp.zeros((bub, blk), F32)
+    group_blocks = 2 * group_pairs
+    filled = group_blocks * bub
+    column = lax.broadcasted_iota(jnp.int32, (blk, blk), 1)
+    member = lax.broadcasted_iota(jnp.int32, (filled, blk), 0) // bub
+
+    def group_of(ref, g):
+        return jnp.concatenate(
+            [ref[:, pl.ds((g * group_blocks + r) * blk, blk)] for r in range(group_blocks)], axis=0
+        )
+
+    def filled_out(held):
+        if filled == blk:
+            return held
+        return jnp.concatenate([held, jnp.zeros((blk - filled, held.shape[1]), F32)], axis=0)
+
+    def take(total, got, wanted):
         for b in range(bub):
-            got = dot_nt(left, right_of(b))
-            even = jnp.where(line == b, got[:bub, :blk], even)
-            odd = jnp.where(line == b, got[bub:, blk:], odd)
-        return jnp.concatenate([even, odd], axis=0)
-
-    def stacked(ref, q):
-        first, second = cols(2 * q * blk, blk), cols((2 * q + 1) * blk, blk)
-        return jnp.concatenate([ref[:, first], ref[:, second]], axis=0)
-
-    def near_block(b, q):
-        return jnp.concatenate(
-            [
-                jnp.concatenate([near_v[b, 2 * q + o, s] for s in range(slots)], axis=1)
-                for o in range(2)
-            ],
-            axis=0,
-        )
-
-    def inv_block(b, q):
-        return jnp.concatenate([inv_v[b, 2 * q], inv_v[b, 2 * q + 1]], axis=0)
-
-    both_tint = jnp.concatenate([tint, tint], axis=0)
-
-    def solve(phase, old_ref, some):
-        rests = []
-        for q in some:
-            left = jnp.concatenate(
-                [
-                    picked[pl.ds(pl.multiple_of((s * rows + 2 * q) * bub, 16), 16), :].astype(BF16)
-                    for s in range(slots)
-                ],
-                axis=1,
+            hit = wanted(b)
+            total = jnp.where(hit, got[b * blk : (b + 1) * blk], total)
+        return total
+
+    def solve(phase, old_ref, g):
+        first = g * group_blocks
+        held = jnp.concatenate(
+            [picked[pl.ds((s * rows + first) * bub, filled), :] for s in range(slots)], axis=1
+        )
+        held = filled_out(held).astype(BF16)
+
+        def near_step(t, total):
+            q = g * group_pairs + t
+            if phase == 0:
+                near_copy(q).wait()
+            for o in range(2):
+                r = 2 * q + o
+                blocks = jnp.concatenate(
+                    [near_v[:, r, s].reshape(bub * blk, blk) for s in range(slots)], axis=1
+                )
+                base = (2 * t + o) * bub
+                total = take(total, dot_nt(blocks, held), lambda b: column == base + b)
+            return total
+
+        near = lax.fori_loop(0, group_pairs, near_step, jnp.zeros((blk, blk), F32))
+        near = near.T[:filled]
+        rest = group_of(rhs_ref, g) - near - group_of(far_v, g)
+
+        def solve_step(t, total):
+            q = g * group_pairs + t
+            if phase == 0:
+                inv_copy(q).wait()
+            blocks = jnp.concatenate(
+                [inv_v[:, 2 * q + o].reshape(bub * blk, blk) for o in range(2)], axis=1
             )
-            near = by_bubble(left, lambda b: near_block(b, q))
-            rests.append((stacked(rhs_ref, q) - near - stacked(far_v, q)).astype(BF16))
-        news = []
-        for q, rest in zip(some, rests):
-            updated = by_bubble(rest, lambda b: inv_block(b, q))
-            news.append(jnp.where(both_tint == phase, updated, stacked(old_ref, q)))
-        for q, new in zip(some, news):
-            out_ref[:, cols(2 * q * blk, blk)] = new[:bub]
-            out_ref[:, cols((2 * q + 1) * blk, blk)] = new[bub:]
-        return news
+            two = jnp.concatenate(
+                [jnp.where(member == 2 * t + o, rest, 0.0) for o in range(2)], axis=1
+            )
+            got = dot_nt(blocks, filled_out(two).astype(BF16))
+            base = 2 * t * bub
+            return take(
+                total, got, lambda b: (column == base + b) | (column == base + bub + b)
+            )
+
+        updated = lax.fori_loop(0, group_pairs, solve_step, jnp.zeros((blk, blk), F32))
+        updated = updated.T[:filled]
+        tints = jnp.concatenate([tint] * group_blocks, axis=0)
+        new = jnp.where(tints == phase, updated, group_of(old_ref, g))
+        for r in range(group_blocks):
+            out_ref[:, (first + r) * blk : (first + r + 1) * blk] = new[r * bub : (r + 1) * bub]
+        return new
 
     spread_copy.wait()
     for_peers(lambda *a: dens_arrival(*pieces[0], *a).wait_recv())
     pick(0)
     far_field(0)
-    batch = 2 if group_pairs % 2 == 0 else 1
-
-    def first_colour(t, carry):
-        some = [batch * t + o for o in range(batch)]
-        for q in some:
-            near_copy(q).wait()
-            inv_copy(q).wait()
-        for q, new in zip(some, solve(0, dens_ref, some)):
-            hood[1, rows_of(own_slot, q * 16, 16), :] = new.astype(BF16)
-        return carry
-
-    steps = group_pairs // batch
     for g in range(groups):
-        lax.fori_loop(g * steps, (g + 1) * steps, first_colour, 0)
+        new = solve(0, dens_ref, g)
+        hood[1, rows_of(own_slot, g * group_rows, group_rows), :] = new.astype(BF16)
         for_peers(lambda *a: dens_copy(*pieces[1 + g], *a).start())
 
     send_moments(1, out_ref)
@@ -373,11 +383,8 @@
     pick(1)
     far_field(1)
 
-    def second_colour(t, carry):
-        solve(1, out_ref, [batch * t + o for o in range(batch)])
-        return carry
-
-    lax.fori_loop(0, pairs // batch, second_colour, 0)
+    for g in range(groups):
+        solve(1, out_ref, g)
 
     for piece in pieces:
         for_peers(lambda *a: dens_copy(*piece, *a).wait_send())

time: 51.6 us -> 58.1 us (1.13)
  Pallas kernels: 49.9 us -> 56.4 us
    pallas_call x1, Pallas kernels: 49.9 us -> 56.4 us  [per_device(): pl.pallas_call(functools.partial(kernel, nbub, npan, groups), out_shape=j...]
where the time goes in v3:
time: 58.1 us; the launch traced here: 57.9 us
  Pallas kernels  56.4 us (97%)
  local copies, waits for them, and re-layouts  1.54 us (3%)
    pallas_call x1, Pallas kernels, per_device(): pl.pallas_call(functools.partial(kernel, nbub, npan, groups), out_shape=j...  56.4 us
    unnamed x1, local copies, waits for them, and re-layouts  1.54 us

profile of v3, /device:TPU:0, one launch (start us, length us, event | category | flops | bytes accessed | tf_op | source)
XLA Modules:
  0.0 57.9 jit_solution(1471446631543550406)
XLA Ops:
  0.0 56.4 %shard_map.109 = f32[8,3072]{1,0:T(8,128)} custom-call(f32[8,3072]{1,0:T(8,128)} %dens_ref.1, f32[8,3072]{1,0:T(8,128)} %rhs_ref.1, bf16[8,24,128,128]{3,2,1,0:T(8,128)(2,1)} %inv_hbm.1, bf16[8,24,4,128,128]{4,3,2,1,0:T(8,128)(2,1)} %near_hbm.1, s32[8,4,24]{2,1,0:T(4,128)} %bitcast.6, s32[8,4,24]{2,1,0:T(4,128)} %bitcast.7, s32[8,24]{1,0:T(8,128)} %count_ref.1, ...), custom_call_target="tpu_custom_call" | custom-call | tf_op jit(solution)/shard_map/pallas_call | solution.py:422
  56.4 1.5 %copy.13 = f32[8,3072]{1,0:T(8,128)} copy(f32[8,3072]{1,0:T(8,128)} %shard_map.109) | data formatting | bytes 196608

commit v4 on v2

--- a/solution.py
+++ b/solution.py
@@ -298,14 +298,19 @@
 
         lax.fori_loop(0, 2, step, 0)
 
-    def by_bubble(left, right_of):
-        even = jnp.zeros((bub, blk), F32)
-        odd = jnp.zeros((bub, blk), F32)
-        for b in range(bub):
-            got = dot_nt(left, right_of(b))
-            even = jnp.where(line == b, got[:bub, :blk], even)
-            odd = jnp.where(line == b, got[bub:, blk:], odd)
-        return jnp.concatenate([even, odd], axis=0)
+    line_two = lax.rem(lax.broadcasted_iota(jnp.int32, (2 * bub, blk), 0), bub)
+
+    def by_bubble(parts, right_of, count):
+        total = None
+        for first in range(0, bub, count):
+            some = range(first, first + count)
+            left = jnp.concatenate(
+                [jnp.where(line_two == b, part, 0.0) for b in some for part in parts], axis=1
+            )
+            right = jnp.concatenate([right_of(b) for b in some], axis=1)
+            got = dot_nt(left.astype(BF16), right)
+            total = got if total is None else total + got
+        return jnp.concatenate([total[:bub, :blk], total[bub:, blk:]], axis=0)
 
     def stacked(ref, q):
         first, second = cols(2 * q * blk, blk), cols((2 * q + 1) * blk, blk)
@@ -328,18 +333,15 @@
     def solve(phase, old_ref, some):
         rests = []
         for q in some:
-            left = jnp.concatenate(
-                [
-                    picked[pl.ds(pl.multiple_of((s * rows + 2 * q) * bub, 16), 16), :].astype(BF16)
-                    for s in range(slots)
-                ],
-                axis=1,
-            )
-            near = by_bubble(left, lambda b: near_block(b, q))
-            rests.append((stacked(rhs_ref, q) - near - stacked(far_v, q)).astype(BF16))
+            parts = [
+                picked[pl.ds(pl.multiple_of((s * rows + 2 * q) * bub, 16), 16), :]
+                for s in range(slots)
+            ]
+            near = by_bubble(parts, lambda b: near_block(b, q), 2)
+            rests.append(stacked(rhs_ref, q) - near - stacked(far_v, q))
         news = []
         for q, rest in zip(some, rests):
-            updated = by_bubble(rest, lambda b: inv_block(b, q))
+            updated = by_bubble([rest], lambda b: inv_block(b, q), bub)
             news.append(jnp.where(both_tint == phase, updated, stacked(old_ref, q)))
         for q, new in zip(some, news):
             out_ref[:, cols(2 * q * blk, blk)] = new[:bub]

time: 51.6 us -> 51.8 us (level)
  no operation moved by 1% of the time
where the time goes in v4:
time: 51.8 us; the launch traced here: 51.6 us
  Pallas kernels  50.1 us (97%)
  local copies, waits for them, and re-layouts  1.54 us (3%)
    pallas_call x1, Pallas kernels, per_device(): pl.pallas_call(functools.partial(kernel, nbub, npan, groups), out_shape=j...  50.1 us
    unnamed x1, local copies, waits for them, and re-layouts  1.54 us

profile of v4, /device:TPU:0, one launch (start us, length us, event | category | flops | bytes accessed | tf_op | source)
XLA Modules:
  0.0 51.6 jit_solution(13271734569163365545)
XLA Ops:
  0.0 50.1 %shard_map.109 = f32[8,3072]{1,0:T(8,128)} custom-call(f32[8,3072]{1,0:T(8,128)} %dens_ref.1, f32[8,3072]{1,0:T(8,128)} %rhs_ref.1, bf16[8,24,128,128]{3,2,1,0:T(8,128)(2,1)} %inv_hbm.1, bf16[8,24,4,128,128]{4,3,2,1,0:T(8,128)(2,1)} %near_hbm.1, s32[8,4,24]{2,1,0:T(4,128)} %bitcast.6, s32[8,4,24]{2,1,0:T(4,128)} %bitcast.7, s32[8,24]{1,0:T(8,128)} %count_ref.1, ...), custom_call_target="tpu_custom_call" | custom-call | tf_op jit(solution)/shard_map/pallas_call | solution.py:417
  50.1 1.5 %copy.13 = f32[8,3072]{1,0:T(8,128)} copy(f32[8,3072]{1,0:T(8,128)} %shard_map.109) | data formatting | bytes 196608

commit v5 on v4

--- a/solution.py
+++ b/solution.py
@@ -46,7 +46,10 @@
     near_sem,
     inv_sem,
     map_sem,
-    dens_send,
+    halo_send,
+    cross_send,
+    core_send,
+    direct_send,
     dens_recv,
     part_send,
     part_recv,
@@ -146,28 +149,107 @@
     sides = (me_b > 0).astype(jnp.int32) + (me_b < nbub - 1).astype(jnp.int32)
     pl.semaphore_wait(barrier, npan - 1 + npan * sides + nbub - 1)
 
-    def dens_copy(sem, phase, first, size, j, side, p, other):
-        piece = hood.at[phase, rows_of(own_slot, first, size)]
-        back = (2 - side) * npan + me_p
+    group_rows = group_pairs * 16
+    pieces = [(0, 0, chunk)] + [(1, g * group_rows, group_rows) for g in range(groups)]
+    last = groups
+    parity = lax.rem(me_p, 2)
+    partner = me_p + 1 - 2 * parity
+
+    def dens_copy(e, source, target, send, other, p):
+        phase, first, size = pieces[e]
         return pltpu.make_async_remote_copy(
-            src_ref=piece,
-            dst_ref=hood.at[phase, rows_of(back, first, size)],
-            send_sem=dens_send.at[sem, j],
-            recv_sem=dens_recv.at[sem, back],
+            src_ref=hood.at[phase, rows_of(source, first, size)],
+            dst_ref=hood.at[phase, rows_of(target, first, size)],
+            send_sem=send,
+            recv_sem=dens_recv.at[e, target],
             device_id=(other, p),
             device_id_type=MESH,
         )
 
-    def dens_arrival(sem, phase, first, size, j, side, p, other):
-        piece = hood.at[phase, rows_of(j, first, size)]
-        return pltpu.make_async_remote_copy(
-            src_ref=piece,
-            dst_ref=piece,
-            send_sem=dens_send.at[sem, j],
-            recv_sem=dens_recv.at[sem, j],
-            device_id=(other, p),
-            device_id_type=MESH,
-        )
+    def arrive(e, slot):
+        dens_copy(e, slot, slot, direct_send.at[0], me_b, partner).wait_recv()
+
+    def where_side(side, do):
+        if side == 1:
+            do()
+        else:
+            pl.when(me_b > 0 if side == 0 else me_b < nbub - 1)(do)
+
+    def halo(e, act):
+        for side in (0, 2):
+            target = (2 - side) * npan + me_p
+            where_side(
+                side,
+                lambda: act(
+                    dens_copy(
+                        e, own_slot, target, halo_send.at[e, side], me_b + side - 1, me_p
+                    )
+                ),
+            )
+
+    def cross(e, side, act):
+        slot = side * npan + me_p
+        for i in range(npan // 2):
+            p = 2 * i + parity
+
+            @pl.when(p != me_p)
+            def _():
+                act(dens_copy(e, slot, slot, cross_send.at[e, side, i], me_b, p))
+
+    def core(e, slot, act):
+        act(dens_copy(e, slot, slot, core_send.at[e, slot], me_b, partner))
+
+    def first_hop(e):
+        halo(e, lambda c: c.start())
+        cross(e, 1, lambda c: c.start())
+        core(e, own_slot, lambda c: c.start())
+
+    def second_hop(e):
+        for side in (0, 2):
+
+            def pass_on():
+                slot = side * npan + me_p
+                arrive(e, slot)
+                cross(e, side, lambda c: c.start())
+                core(e, slot, lambda c: c.start())
+
+            where_side(side, pass_on)
+
+    def third_hop(e):
+        for side in (1, 0, 2):
+            for i in range(npan // 2):
+                p = 2 * i + parity
+
+                def pass_on():
+                    slot = side * npan + p
+                    arrive(e, slot)
+                    core(e, slot, lambda c: c.start())
+
+                where_side(side, lambda: pl.when(p != me_p)(pass_on))
+
+    def last_arrivals(e):
+        for side in (1, 0, 2):
+            for i in range(npan // 2):
+                slot = side * npan + 2 * i + 1 - parity
+                where_side(side, lambda: arrive(e, slot))
+
+    def sends_done(e):
+        halo(e, lambda c: c.wait_send())
+        for side in range(3):
+
+            def done():
+                cross(e, side, lambda c: c.wait_send())
+                for i in range(npan // 2):
+                    core(e, side * npan + 2 * i + parity, lambda c: c.wait_send())
+
+            where_side(side, done)
+
+    def direct(act):
+        def one(j, side, p, other):
+            target = (2 - side) * npan + me_p
+            act(dens_copy(last, own_slot, target, direct_send.at[j], other, p))
+
+        for_peers(one)
 
     def part_copy(phase, slot, p):
         return pltpu.make_async_remote_copy(
@@ -189,10 +271,7 @@
             device_id_type=MESH,
         )
 
-    group_rows = group_pairs * 16
-    pieces = [(0, 0, 0, chunk)] + [(1 + g, 1, g * group_rows, group_rows) for g in range(groups)]
-
-    for_peers(lambda *a: dens_copy(*pieces[0], *a).start())
+    first_hop(0)
 
     lane = lax.broadcasted_iota(jnp.int32, (bub, lanes), 1)
     row = lax.broadcasted_iota(jnp.int32, (bub, lanes), 0)
@@ -256,7 +335,10 @@
             onehot[mine_rows, c * 128 : (c + 1) * 128] = jnp.where(hit, 1.0, 0.0).astype(BF16)
         return carry
 
-    lax.fori_loop(0, bub, build, 0)
+    lax.fori_loop(0, bub // 2, build, 0)
+    second_hop(0)
+    lax.fori_loop(bub // 2, bub, build, 0)
+    third_hop(0)
 
     which = lax.broadcasted_iota(jnp.int32, (bub, nbub * bub), 1)
     mine = which == me_b * bub + lax.broadcasted_iota(jnp.int32, (bub, nbub * bub), 0)
@@ -349,7 +431,7 @@
         return news
 
     spread_copy.wait()
-    for_peers(lambda *a: dens_arrival(*pieces[0], *a).wait_recv())
+    last_arrivals(0)
     pick(0)
     far_field(0)
     batch = 2 if group_pairs % 2 == 0 else 1
@@ -364,14 +446,27 @@
         return carry
 
     steps = group_pairs // batch
-    for g in range(groups):
-        lax.fori_loop(g * steps, (g + 1) * steps, first_colour, 0)
-        for_peers(lambda *a: dens_copy(*pieces[1 + g], *a).start())
-
+    total_steps = groups * steps
+
+    def first_steps(t, carry):
+        first_colour(t, carry)
+        for g in range(groups - 1):
+            for hop, do in enumerate((first_hop, second_hop, third_hop)):
+                if (g + 1) * steps - 1 + hop < total_steps:
+                    pl.when(t == (g + 1) * steps - 1 + hop)(functools.partial(do, 1 + g))
+        return carry
+
+    lax.fori_loop(0, total_steps, first_steps, 0)
+    direct(lambda c: c.start())
     send_moments(1, out_ref)
     pass_moments(1)
-    for g in range(groups):
-        for_peers(lambda *a: dens_arrival(*pieces[1 + g], *a).wait_recv())
+    for g in range(groups - 1):
+        for hop, do in enumerate((first_hop, second_hop, third_hop)):
+            if (g + 1) * steps - 1 + hop >= total_steps:
+                do(1 + g)
+    for g in range(groups - 1):
+        last_arrivals(1 + g)
+    for_peers(lambda j, side, p, other: arrive(last, j))
     pick(1)
     far_field(1)
 
@@ -381,8 +476,9 @@
 
     lax.fori_loop(0, pairs // batch, second_colour, 0)
 
-    for piece in pieces:
-        for_peers(lambda *a: dens_copy(*piece, *a).wait_send())
+    for e in range(groups):
+        sends_done(e)
+    direct(lambda c: c.wait_send())
     for phase in range(2):
         for_others(npan, me_p, lambda p: part_copy(phase, me_p, p).wait_send())
         for_others(nbub, me_b, lambda b: mom_copy_to(phase, me_b, b).wait_send())
@@ -434,7 +530,10 @@
             dma((pairs,)),
             dma((pairs,)),
             dma((2,)),
+            dma((1 + groups, 3)),
+            dma((1 + groups, 3, npan // 2)),
             dma((1 + groups, 3 * npan)),
+            dma((3 * npan,)),
             dma((1 + groups, 3 * npan)),
             dma((2, npan)),
             dma((2, npan)),

time: 51.8 us -> 56 us (1.081)
  Pallas kernels: 50.1 us -> 54.3 us
    pallas_call x1, Pallas kernels: 50.1 us -> 54.3 us  [per_device(): pl.pallas_call(functools.partial(kernel, nbub, npan, groups), out_shape=j...]
where the time goes in v5:
time: 56 us; the launch traced here: 55.9 us
  Pallas kernels  54.3 us (97%)
  local copies, waits for them, and re-layouts  1.54 us (3%)
    pallas_call x1, Pallas kernels, per_device(): pl.pallas_call(functools.partial(kernel, nbub, npan, groups), out_shape=j...  54.3 us
    unnamed x1, local copies, waits for them, and re-layouts  1.54 us

profile of v5, /device:TPU:0, one launch (start us, length us, event | category | flops | bytes accessed | tf_op | source)
XLA Modules:
  0.0 55.9 jit_solution(8015814749654271034)
XLA Ops:
  0.0 54.3 %shard_map.109 = f32[8,3072]{1,0:T(8,128)} custom-call(f32[8,3072]{1,0:T(8,128)} %dens_ref.1, f32[8,3072]{1,0:T(8,128)} %rhs_ref.1, bf16[8,24,128,128]{3,2,1,0:T(8,128)(2,1)} %inv_hbm.1, bf16[8,24,4,128,128]{4,3,2,1,0:T(8,128)(2,1)} %near_hbm.1, s32[8,4,24]{2,1,0:T(4,128)} %bitcast.6, s32[8,4,24]{2,1,0:T(4,128)} %bitcast.7, s32[8,24]{1,0:T(8,128)} %count_ref.1, ...), custom_call_target="tpu_custom_call" | custom-call | tf_op jit(solution)/shard_map/pallas_call | solution.py:513
  54.3 1.5 %copy.13 = f32[8,3072]{1,0:T(8,128)} copy(f32[8,3072]{1,0:T(8,128)} %shard_map.109) | data formatting | bytes 196608

commit v6 on v4

--- a/solution.py
+++ b/solution.py
@@ -316,14 +316,21 @@
         first, second = cols(2 * q * blk, blk), cols((2 * q + 1) * blk, blk)
         return jnp.concatenate([ref[:, first], ref[:, second]], axis=0)
 
+    ones = jnp.ones((2 * bub, blk), F32)
+
     def near_block(b, q):
-        return jnp.concatenate(
-            [
-                jnp.concatenate([near_v[b, 2 * q + o, s] for s in range(slots)], axis=1)
-                for o in range(2)
-            ],
-            axis=0,
-        )
+        both = []
+        for o in range(2):
+            terms = []
+            for s in range(slots):
+                at = (s * rows + 2 * q + o) * bub + b
+                source = jnp.broadcast_to(picked[pl.ds(at, 1), :], (16, blk)).astype(BF16)
+                blocks = near_v[b, 2 * q + o, s].reshape(blk // 16, 16, blk)
+                terms.append(blocks * source[None])
+            while len(terms) > 1:
+                terms = [sum(terms[i + 1 : i + 2], terms[i]) for i in range(0, len(terms), 2)]
+            both.append(terms[0].reshape(blk, blk))
+        return jnp.concatenate(both, axis=0)
 
     def inv_block(b, q):
         return jnp.concatenate([inv_v[b, 2 * q], inv_v[b, 2 * q + 1]], axis=0)
@@ -333,11 +340,7 @@
     def solve(phase, old_ref, some):
         rests = []
         for q in some:
-            parts = [
-                picked[pl.ds(pl.multiple_of((s * rows + 2 * q) * bub, 16), 16), :]
-                for s in range(slots)
-            ]
-            near = by_bubble(parts, lambda b: near_block(b, q), 2)
+            near = by_bubble([ones], lambda b: near_block(b, q), 2)
             rests.append(stacked(rhs_ref, q) - near - stacked(far_v, q))
         news = []
         for q, rest in zip(some, rests):

time: 51.8 us -> 45.6 us (0.88)
  Pallas kernels: 50.1 us -> 43.8 us
    pallas_call x1, Pallas kernels: 50.1 us -> 43.8 us  [per_device(): pl.pallas_call(functools.partial(kernel, nbub, npan, groups), out_shape=j...]
where the time goes in v6:
time: 45.6 us; the launch traced here: 45.4 us
  Pallas kernels  43.8 us (96%)
  local copies, waits for them, and re-layouts  1.54 us (3%)
    pallas_call x1, Pallas kernels, per_device(): pl.pallas_call(functools.partial(kernel, nbub, npan, groups), out_shape=j...  43.8 us
    unnamed x1, local copies, waits for them, and re-layouts  1.54 us

profile of v6, /device:TPU:0, one launch (start us, length us, event | category | flops | bytes accessed | tf_op | source)
XLA Modules:
  0.0 45.4 jit_solution(9076775363473829163)
XLA Ops:
  0.0 43.8 %shard_map.109 = f32[8,3072]{1,0:T(8,128)} custom-call(f32[8,3072]{1,0:T(8,128)} %dens_ref.1, f32[8,3072]{1,0:T(8,128)} %rhs_ref.1, bf16[8,24,128,128]{3,2,1,0:T(8,128)(2,1)} %inv_hbm.1, bf16[8,24,4,128,128]{4,3,2,1,0:T(8,128)(2,1)} %near_hbm.1, s32[8,4,24]{2,1,0:T(4,128)} %bitcast.6, s32[8,4,24]{2,1,0:T(4,128)} %bitcast.7, s32[8,24]{1,0:T(8,128)} %count_ref.1, ...), custom_call_target="tpu_custom_call" | custom-call | tf_op jit(solution)/shard_map/pallas_call | solution.py:420
  43.8 1.5 %copy.13 = f32[8,3072]{1,0:T(8,128)} copy(f32[8,3072]{1,0:T(8,128)} %shard_map.109) | data formatting | bytes 196608

commit v7 on v6

--- a/solution.py
+++ b/solution.py
@@ -327,9 +327,8 @@
                 source = jnp.broadcast_to(picked[pl.ds(at, 1), :], (16, blk)).astype(BF16)
                 blocks = near_v[b, 2 * q + o, s].reshape(blk // 16, 16, blk)
                 terms.append(blocks * source[None])
-            while len(terms) > 1:
-                terms = [sum(terms[i + 1 : i + 2], terms[i]) for i in range(0, len(terms), 2)]
-            both.append(terms[0].reshape(blk, blk))
+            terms = [sum(terms[i + 1 : i + 2], terms[i]) for i in range(0, slots, 2)]
+            both.append(jnp.concatenate([term.reshape(blk, blk) for term in terms], axis=1))
         return jnp.concatenate(both, axis=0)
 
     def inv_block(b, q):
@@ -340,7 +339,7 @@
     def solve(phase, old_ref, some):
         rests = []
         for q in some:
-            near = by_bubble([ones], lambda b: near_block(b, q), 2)
+            near = by_bubble([ones] * ((slots + 1) // 2), lambda b: near_block(b, q), 1)
             rests.append(stacked(rhs_ref, q) - near - stacked(far_v, q))
         news = []
         for q, rest in zip(some, rests):
@@ -355,7 +354,7 @@
     for_peers(lambda *a: dens_arrival(*pieces[0], *a).wait_recv())
     pick(0)
     far_field(0)
-    batch = 2 if group_pairs % 2 == 0 else 1
+    batch = 4 if group_pairs % 4 == 0 else 1
 
     def first_colour(t, carry):
         some = [batch * t + o for o in range(batch)]

time: 45.6 us -> 45 us (0.987)
  Pallas kernels: 43.8 us -> 43.3 us
    pallas_call x1, Pallas kernels: 43.8 us -> 43.3 us  [per_device(): pl.pallas_call(functools.partial(kernel, nbub, npan, groups), out_shape=j...]
where the time goes in v7:
time: 45 us; the launch traced here: 44.8 us
  Pallas kernels  43.3 us (96%)
  local copies, waits for them, and re-layouts  1.54 us (3%)
    pallas_call x1, Pallas kernels, per_device(): pl.pallas_call(functools.partial(kernel, nbub, npan, groups), out_shape=j...  43.3 us
    unnamed x1, local copies, waits for them, and re-layouts  1.54 us

profile of v7, /device:TPU:0, one launch (start us, length us, event | category | flops | bytes accessed | tf_op | source)
XLA Modules:
  0.0 44.8 jit_solution(2815026418462686852)
XLA Ops:
  0.0 43.3 %shard_map.109 = f32[8,3072]{1,0:T(8,128)} custom-call(f32[8,3072]{1,0:T(8,128)} %dens_ref.1, f32[8,3072]{1,0:T(8,128)} %rhs_ref.1, bf16[8,24,128,128]{3,2,1,0:T(8,128)(2,1)} %inv_hbm.1, bf16[8,24,4,128,128]{4,3,2,1,0:T(8,128)(2,1)} %near_hbm.1, s32[8,4,24]{2,1,0:T(4,128)} %bitcast.6, s32[8,4,24]{2,1,0:T(4,128)} %bitcast.7, s32[8,24]{1,0:T(8,128)} %count_ref.1, ...), custom_call_target="tpu_custom_call" | custom-call | tf_op jit(solution)/shard_map/pallas_call | solution.py:419
  43.3 1.5 %copy.13 = f32[8,3072]{1,0:T(8,128)} copy(f32[8,3072]{1,0:T(8,128)} %shard_map.109) | data formatting | bytes 196608
